TPU v7x, 32 devices: a whole 2x2x4 slice. The times are simulated.
32 devices in a mesh: image: 8 (over y, x, core), space: 4 (over z).
Axes of the slice: x: 2, y: 2, z: 4, core: 2. Of those that a mesh axis runs over, the one named last changes fastest.
Arguments:
- coords: float32 [16, 3, 32768], P('image', None, 'space'), may hold values from -16 to 16
- ref_coords: float32 [3, 32768], P(None, 'space'), may hold values from -4 to 4
- restraint: float32 [32768], P('space'), may hold values from 0.5 to 5
- atom_types: int32 [32768], P('space'), may hold values from 0 to 63
- well_table: float32 [64], replicated, may hold values from 0.3 to 1.5
- radius_table: float32 [64], replicated, may hold values from 0.4 to 1
- tile_lists: int32 [16, 4, 256], P('image', None, 'space'), may hold values from 0 to 79
- halo_index: int32 [16, 2, 4096], P('image', None, 'space'), may hold values from 0 to 8191
Outputs:
- neb_force: float32 [16, 3, 32768], P('image', None, 'space')
- energies: float32 [16], P('image')
All inputs are finite; a program needn't handle non-finite values.
Results may differ from a plain program's by a relative error of at most 0.0001.
Values sent between devices are 32-bit elements; how exact they have to be, the bound alone decides.
A program may use at most 64 MiB of HBM per device.

v0:
```python
import jax
import jax.numpy as jnp
from jax import lax
from jax.sharding import PartitionSpec as P

TILE = 128


soft_core = 1.0
spring_k = 2.0
small_eps = 1e-06


def extended_2(x, sides, width):
    for axis, dim in sides:
        devices, length = (lax.axis_size(axis), x.shape[dim])
        up = [(i, (i + 1) % devices) for i in range(devices - 1)]
        down = [(j, i) for i, j in up]
        last = lax.slice_in_dim(x, length - width, length, axis=dim)
        leading = lax.slice_in_dim(x, 0, width, axis=dim)
        before = lax.ppermute(last, axis, up)
        after = lax.ppermute(leading, axis, down)
        x = jnp.concatenate([before, x, after], axis=dim)
    return x


def pair_terms(own, partner):
    delta = own[:3, ..., :, None] - partner[:3, ..., None, :]
    dist_sq = jnp.sum(delta * delta, axis=0)
    reach = own[4, ..., :, None] + partner[4, ..., None, :]
    reach_sq = reach * reach
    ratio = reach_sq / (dist_sq + soft_core * reach_sq)
    cubed = ratio * ratio * ratio
    strength = own[3, ..., :, None] * partner[3, ..., None, :]
    energy = jnp.sum(4.0 * strength * (cubed * cubed - cubed), axis=(-2, -1))
    coeff = 24.0 * strength * (2.0 * cubed * cubed - cubed) * ratio / reach_sq
    force = jnp.sum(coeff[None] * delta, axis=-1)
    return (force, energy)


def image_total(values):
    return jnp.sum(values, axis=(1, 2))


def body(
    coords, ref_coords, restraint, atom_types, well_table, radius_table, tile_lists, halo_index
):
    img_local, _, atoms_local = coords.shape
    tiles_local = atoms_local // TILE
    kinds = well_table.shape[0]
    table = jnp.stack([well_table, radius_table])
    onehot = (atom_types[None, :] == jnp.arange(kinds, dtype=jnp.int32)[:, None]).astype(
        jnp.float32
    )
    params = jnp.dot(table, onehot, precision=lax.Precision.HIGHEST)
    feats = jnp.concatenate(
        [coords, jnp.broadcast_to(params[None], (img_local, 2, atoms_local))], axis=1
    )
    pick_atoms = jax.vmap(lambda source, index: source[:, index])
    pick_tiles = jax.vmap(lambda source, index: source[:, index, :])
    wide = extended_2(feats, (("space", 2),), atoms_local)
    lower = pick_atoms(wide[:, :, :atoms_local], halo_index[:, 0])
    upper = pick_atoms(wide[:, :, 2 * atoms_local :], halo_index[:, 1])
    extended = jnp.concatenate([feats, lower, upper], axis=2).reshape(img_local, 5, -1, TILE)
    own = feats.reshape(img_local, 5, tiles_local, TILE).transpose(1, 0, 2, 3)

    def add_partner(carry, index):
        partner = pick_tiles(extended, index).transpose(1, 0, 2, 3)
        force, energy = pair_terms(own, partner)
        return ((carry[0] + force, carry[1] + jnp.sum(energy, axis=1)), None)

    start = (
        jnp.zeros((3, img_local, tiles_local, TILE), jnp.float32),
        jnp.zeros((img_local,), jnp.float32),
    )
    (pair_force, pair_energy), _ = lax.scan(
        add_partner, start, jnp.transpose(tile_lists, (1, 0, 2))
    )
    pair_force = pair_force.transpose(1, 0, 2, 3).reshape(img_local, 3, atoms_local)
    offset = coords - ref_coords[None]
    forces = pair_force - restraint[None, None] * offset
    local_energy = 0.5 * pair_energy + 0.5 * image_total(restraint[None, None] * offset * offset)
    rims = extended_2(coords, (("image", 0),), 1)
    ahead = rims[2:] - coords
    behind = coords - rims[:-2]
    ahead_sq, behind_sq, cross, force_ahead, force_behind, energy_sum = lax.psum(
        (
            image_total(ahead * ahead),
            image_total(behind * behind),
            image_total(ahead * behind),
            image_total(forces * ahead),
            image_total(forces * behind),
            local_energy,
        ),
        "space",
    )
    ahead_norm = jnp.sqrt(ahead_sq + small_eps)
    behind_norm = jnp.sqrt(behind_sq + small_eps)
    tan_sq = (
        ahead_sq / (ahead_norm * ahead_norm)
        + 2.0 * cross / (ahead_norm * behind_norm)
        + behind_sq / (behind_norm * behind_norm)
    )
    tan_norm = jnp.sqrt(tan_sq + small_eps)
    ahead_len = ahead_norm[:, None, None]
    behind_len = behind_norm[:, None, None]
    tan_len = tan_norm[:, None, None]
    unit = (ahead / ahead_len + behind / behind_len) / tan_len
    along = ((force_ahead / ahead_norm + force_behind / behind_norm) / tan_norm)[:, None, None]
    banded = forces - along * unit + spring_k * (ahead_len - behind_len) * unit
    total_images = img_local * lax.axis_size("image")
    order = lax.axis_index("image") * img_local + jnp.arange(img_local, dtype=jnp.int32)
    ends = ((order == 0) | (order == total_images - 1))[:, None, None]
    neb_force = jnp.where(ends, forces, banded)
    energies = energy_sum / (atoms_local * lax.axis_size("space"))
    return (neb_force, energies)


def solution(mesh):
    in_specs = (
        P("image", None, "space"),
        P(None, "space"),
        P("space"),
        P("space"),
        P(),
        P(),
        P("image", None, "space"),
        P("image", None, "space"),
    )
    out_specs = (P("image", None, "space"), P("image"))
    return jax.shard_map(body, mesh=mesh, in_specs=in_specs, out_specs=out_specs, check_vma=False)
```

profile of v0, /device:TPU:0, one launch (start us, length us, event | category | flops | bytes accessed | tf_op | source)
XLA Modules:
  0.0 236.8 jit_solution(5420845449610132567)
XLA Ops:
  0.6 1.5 fusion.11
  3.3 1.3 collective-permute-start.1
  4.6 5.6 %collective-permute-start = (f32[2,5,8192]{2,0,1:T(2,128)S(1)}, f32[2,5,8192]{2,0,1:T(2,128)S(1)}, u32[]{:S(2)}, u32[]{:S(2)}) collective-permute-start(f32[2,5,8192]{2,0,1:T(2,128)S(1)} %pad_maximum_fusion.1), channel_id=1, source_target_pairs={{0,1},{1,2},{2,3},{4,5},{5,6},{6,7},{8,9},{9,10},{10,11},{12,13},{... | collective-permute-start | bytes 983048 | tf_op jit(solution)/shard_map/ppermute | solution.py:21
  10.2 1.2 fusion.29
  11.4 1.3 collective-permute-start.2
  12.7 3.0 %collective-permute-start.3 = (f32[1,3,8192]{2,0,1:T(1,128)S(1)}, f32[1,3,8192]{2,0,1:T(1,128)S(1)}, u32[]{:S(2)}, u32[]{:S(2)}) collective-permute-start(f32[1,3,8192]{2,0,1:T(1,128)S(1)} %get-tuple-element.117), channel_id=1, source_target_pairs={{0,4},{4,8},{8,12},{12,16},{16,20},{20,24},{24,28},{1,5},{5,9},{9,... | collective-permute-start | bytes 294920 | tf_op jit(solution)/shard_map/ppermute | solution.py:21
  17.6 4.6 %copy.32 = f32[2,5,8192]{1,2,0:T(8,128)} copy(f32[2,5,8192]{2,0,1:T(2,128)S(1)} %collective-permute-done.1) | data formatting | bytes 655360 | tf_op jit(solution)/shard_map/ppermute | solution.py:22
  22.2 20.5 %gather_fusion.2 = f32[2048,5]{1,0:T(8,128)S(1)} fusion(f32[2,5,8192]{1,2,0:T(8,128)} %copy.32, s32[2048]{0:T(1024)S(1)} %bitcast.49), kind=kCustom, calls=%fused_computation.2 | custom fusion | bytes 98304 | tf_op jit(solution)/shard_map/vmap()/gather | solution.py:59
  43.1 4.7 %copy.30 = f32[2,5,8192]{1,2,0:T(8,128)} copy(f32[2,5,8192]{2,0,1:T(2,128)S(1)} %collective-permute-done) | data formatting | bytes 655360 | tf_op jit(solution)/shard_map/ppermute | solution.py:21
  47.7 20.5 %gather_fusion.1 = f32[2048,5]{1,0:T(8,128)S(1)} fusion(f32[2,5,8192]{1,2,0:T(8,128)} %copy.30, s32[2048]{0:T(1024)S(1)} %bitcast.48), kind=kCustom, calls=%fused_computation.1 | custom fusion | bytes 98304 | tf_op jit(solution)/shard_map/vmap()/gather | solution.py:59
  69.4 154.2 %while.13 = (s32[]{:T(128)}, f32[3,2,64,128]{3,2,1,0:T(8,128)S(1)}, f32[2]{0:T(128)S(1)}, f32[5,2,64,128]{3,2,1,0:T(8,128)S(1)}, s32[4,2,64]{2,1,0:T(2,128)S(1)}...) while((s32[]{:T(128)}, f32[3,2,64,128]{3,2,1,0:T(8,128)S(1)}, f32[2]{0:T(128)S(1)}, ...), condition=%wide.region_4.0_spmd.clone, body=%wide.region_0.4_spmd.clone.sunk | while | flops 75547648 | bytes 37751936 | solution.py:76
  70.7 11.6 %fusion.38 = f32[2,64,128,128]{3,2,1,0:T(8,128)} fusion(f32[3,2,64,128]{3,2,1,0:T(8,128)S(1)} %copy.38, f32[3,2,64,128]{3,2,1,0:T(8,128)S(1)} %slice.76), kind=kLoop, calls=%fused_computation.5.clone.1 | loop fusion | flops 16777216 | bytes 8781824 | tf_op jit(solution)/shard_map/while/body/eval_jaxpr/reduce_sum | solution.py:29
  82.4 10.0 %fusion.39 = (f32[2]{0:T(128)S(1)}, f32[2,64,128,128]{3,2,1,0:T(8,128)S(1)}) fusion(f32[2,64,128]{2,1,0:T(8,128)S(1)} %bitcast.54, f32[2,64,128]{2,1,0:T(8,128)S(1)} %get-tuple-element.169, f32[2,64,128,128]{3,2,1,0:T(8,128)} %fusion.38, f32[2,64,128]{2,1,0:T(8,128)S(1)} %bitcast.55, f32[2,64,128]{2,1,0:T(8,128)S(1)} %get-tuple-element.171), kind=kLoop, calls=%fused_computation.17.clone.1 | loop fusion | flops 39845888 | bytes 17039368 | tf_op jit(solution)/shard_map/while/body/eval_jaxpr/reduce_sum | solution.py:70
  92.4 15.5 %fusion.40 = f32[3,2,64,128]{3,2,1,0:T(8,128)S(1)} fusion(f32[2,64,128,128]{3,2,1,0:T(8,128)S(1)} %get-tuple-element.172, f32[3,2,64,128]{3,2,1,0:T(8,128)S(1)} %copy.38, f32[3,2,64,128]{3,2,1,0:T(8,128)S(1)} %slice.76), kind=kLoop, calls=%fused_computation.6.clone.1 | loop fusion | flops 18825216 | bytes 8978432 | tf_op jit(solution)/shard_map/while/body/eval_jaxpr/reduce_sum | solution.py:37
  109.2 11.6 %fusion.38 = f32[2,64,128,128]{3,2,1,0:T(8,128)} fusion(f32[3,2,64,128]{3,2,1,0:T(8,128)S(1)} %copy.38, f32[3,2,64,128]{3,2,1,0:T(8,128)S(1)} %slice.76), kind=kLoop, calls=%fused_computation.5.clone.1 | loop fusion | flops 16777216 | bytes 8781824 | tf_op jit(solution)/shard_map/while/body/eval_jaxpr/reduce_sum | solution.py:29
  120.9 10.0 %fusion.39 = (f32[2]{0:T(128)S(1)}, f32[2,64,128,128]{3,2,1,0:T(8,128)S(1)}) fusion(f32[2,64,128]{2,1,0:T(8,128)S(1)} %bitcast.54, f32[2,64,128]{2,1,0:T(8,128)S(1)} %get-tuple-element.169, f32[2,64,128,128]{3,2,1,0:T(8,128)} %fusion.38, f32[2,64,128]{2,1,0:T(8,128)S(1)} %bitcast.55, f32[2,64,128]{2,1,0:T(8,128)S(1)} %get-tuple-element.171), kind=kLoop, calls=%fused_computation.17.clone.1 | loop fusion | flops 39845888 | bytes 17039368 | tf_op jit(solution)/shard_map/while/body/eval_jaxpr/reduce_sum | solution.py:70
  130.9 15.5 %fusion.40 = f32[3,2,64,128]{3,2,1,0:T(8,128)S(1)} fusion(f32[2,64,128,128]{3,2,1,0:T(8,128)S(1)} %get-tuple-element.172, f32[3,2,64,128]{3,2,1,0:T(8,128)S(1)} %copy.38, f32[3,2,64,128]{3,2,1,0:T(8,128)S(1)} %slice.76), kind=kLoop, calls=%fused_computation.6.clone.1 | loop fusion | flops 18825216 | bytes 8978432 | tf_op jit(solution)/shard_map/while/body/eval_jaxpr/reduce_sum | solution.py:37
  147.8 11.6 %fusion.38 = f32[2,64,128,128]{3,2,1,0:T(8,128)} fusion(f32[3,2,64,128]{3,2,1,0:T(8,128)S(1)} %copy.38, f32[3,2,64,128]{3,2,1,0:T(8,128)S(1)} %slice.76), kind=kLoop, calls=%fused_computation.5.clone.1 | loop fusion | flops 16777216 | bytes 8781824 | tf_op jit(solution)/shard_map/while/body/eval_jaxpr/reduce_sum | solution.py:29
  159.5 10.0 %fusion.39 = (f32[2]{0:T(128)S(1)}, f32[2,64,128,128]{3,2,1,0:T(8,128)S(1)}) fusion(f32[2,64,128]{2,1,0:T(8,128)S(1)} %bitcast.54, f32[2,64,128]{2,1,0:T(8,128)S(1)} %get-tuple-element.169, f32[2,64,128,128]{3,2,1,0:T(8,128)} %fusion.38, f32[2,64,128]{2,1,0:T(8,128)S(1)} %bitcast.55, f32[2,64,128]{2,1,0:T(8,128)S(1)} %get-tuple-element.171), kind=kLoop, calls=%fused_computation.17.clone.1 | loop fusion | flops 39845888 | bytes 17039368 | tf_op jit(solution)/shard_map/while/body/eval_jaxpr/reduce_sum | solution.py:70
  169.5 15.5 %fusion.40 = f32[3,2,64,128]{3,2,1,0:T(8,128)S(1)} fusion(f32[2,64,128,128]{3,2,1,0:T(8,128)S(1)} %get-tuple-element.172, f32[3,2,64,128]{3,2,1,0:T(8,128)S(1)} %copy.38, f32[3,2,64,128]{3,2,1,0:T(8,128)S(1)} %slice.76), kind=kLoop, calls=%fused_computation.6.clone.1 | loop fusion | flops 18825216 | bytes 8978432 | tf_op jit(solution)/shard_map/while/body/eval_jaxpr/reduce_sum | solution.py:37
  186.3 11.6 %fusion.38 = f32[2,64,128,128]{3,2,1,0:T(8,128)} fusion(f32[3,2,64,128]{3,2,1,0:T(8,128)S(1)} %copy.38, f32[3,2,64,128]{3,2,1,0:T(8,128)S(1)} %slice.76), kind=kLoop, calls=%fused_computation.5.clone.1 | loop fusion | flops 16777216 | bytes 8781824 | tf_op jit(solution)/shard_map/while/body/eval_jaxpr/reduce_sum | solution.py:29
  198.0 10.0 %fusion.39 = (f32[2]{0:T(128)S(1)}, f32[2,64,128,128]{3,2,1,0:T(8,128)S(1)}) fusion(f32[2,64,128]{2,1,0:T(8,128)S(1)} %bitcast.54, f32[2,64,128]{2,1,0:T(8,128)S(1)} %get-tuple-element.169, f32[2,64,128,128]{3,2,1,0:T(8,128)} %fusion.38, f32[2,64,128]{2,1,0:T(8,128)S(1)} %bitcast.55, f32[2,64,128]{2,1,0:T(8,128)S(1)} %get-tuple-element.171), kind=kLoop, calls=%fused_computation.17.clone.1 | loop fusion | flops 39845888 | bytes 17039368 | tf_op jit(solution)/shard_map/while/body/eval_jaxpr/reduce_sum | solution.py:70
  208.0 15.5 %fusion.40 = f32[3,2,64,128]{3,2,1,0:T(8,128)S(1)} fusion(f32[2,64,128,128]{3,2,1,0:T(8,128)S(1)} %get-tuple-element.172, f32[3,2,64,128]{3,2,1,0:T(8,128)S(1)} %copy.38, f32[3,2,64,128]{3,2,1,0:T(8,128)S(1)} %slice.76), kind=kLoop, calls=%fused_computation.6.clone.1 | loop fusion | flops 18825216 | bytes 8978432 | tf_op jit(solution)/shard_map/while/body/eval_jaxpr/reduce_sum | solution.py:37
  225.0 10.3 %all-reduce = (f32[2]{0:T(128)S(1)}, f32[2]{0:T(128)S(1)}, f32[2]{0:T(128)S(1)}, f32[2]{0:T(128)S(1)}, f32[2]{0:T(128)S(1)}, /*index=5*/f32[2]{0:T(128)S(1)}) all-reduce(f32[2]{0:T(128)S(1)} %get-tuple-element.86, f32[2]{0:T(128)S(1)} %get-tuple-element.85, ...), channel_id=1, replica_groups=mesh['image'=8,'space'=4] {'space'}, use_global_device_ids=true, to_apply=%region_8.9 | all-reduce | flops 12 | bytes 96 | tf_op jit(solution)/shard_map/psum | solution.py:86
  (68 shorter events, 12.8 us)
Async XLA Ops:
  3.3 14.3 %collective-permute-start.1 = (f32[2,5,8192]{2,0,1:T(2,128)S(1)}, f32[2,5,8192]{2,0,1:T(2,128)S(1)}, u32[]{:S(2)}, u32[]{:S(2)}) collective-permute-start(f32[2,5,8192]{2,0,1:T(2,128)S(1)} %pad_maximum_fusion.1), channel_id=1, source_target_pairs={{1,0},{2,1},{3,2},{5,4},{6,5},{7,6},{9,8},{10,9},{11,10},{13,12},{... | collective-permute-start | bytes 983048 | tf_op jit(solution)/shard_map/ppermute | solution.py:22
  4.6 38.5 %collective-permute-start = (f32[2,5,8192]{2,0,1:T(2,128)S(1)}, f32[2,5,8192]{2,0,1:T(2,128)S(1)}, u32[]{:S(2)}, u32[]{:S(2)}) collective-permute-start(f32[2,5,8192]{2,0,1:T(2,128)S(1)} %pad_maximum_fusion.1), channel_id=1, source_target_pairs={{0,1},{1,2},{2,3},{4,5},{5,6},{6,7},{8,9},{9,10},{10,11},{12,13},{... | collective-permute-start | bytes 983048 | tf_op jit(solution)/shard_map/ppermute | solution.py:21
  11.4 212.4 %collective-permute-start.2 = (f32[1,3,8192]{2,0,1:T(1,128)S(1)}, f32[1,3,8192]{2,0,1:T(1,128)S(1)}, u32[]{:S(2)}, u32[]{:S(2)}) collective-permute-start(f32[1,3,8192]{2,0,1:T(1,128)S(1)} %get-tuple-element.118), channel_id=1, source_target_pairs={{4,0},{8,4},{12,8},{16,12},{20,16},{24,20},{28,24},{5,1},{9,5},{13... | collective-permute-start | bytes 294920 | tf_op jit(solution)/shard_map/ppermute | solution.py:22
  12.7 211.1 %collective-permute-start.3 = (f32[1,3,8192]{2,0,1:T(1,128)S(1)}, f32[1,3,8192]{2,0,1:T(1,128)S(1)}, u32[]{:S(2)}, u32[]{:S(2)}) collective-permute-start(f32[1,3,8192]{2,0,1:T(1,128)S(1)} %get-tuple-element.117), channel_id=1, source_target_pairs={{0,4},{4,8},{8,12},{12,16},{16,20},{20,24},{24,28},{1,5},{5,9},{9,... | collective-permute-start | bytes 294920 | tf_op jit(solution)/shard_map/ppermute | solution.py:21
  22.2 46.3 %copy-start = (f32[2,3,8192]{2,0,1:T(2,128)S(1)}, f32[2,3,8192]{2,0,1:T(2,128)}, u32[]{:S(2)}) copy-start(f32[2,3,8192]{2,0,1:T(2,128)} %param.10) | copy-start | bytes 589828
  69.4 154.4 %copy-start.1 = (f32[3,8192]{1,0:T(4,128)S(1)}, f32[3,8192]{1,0:T(4,128)}, u32[]{:S(2)}) copy-start(f32[3,8192]{1,0:T(4,128)} %param.11) | copy-start | bytes 294916
  69.4 154.4 %copy-start.2 = (f32[8192]{0:T(1024)S(1)}, f32[8192]{0:T(1024)}, u32[]{:S(2)}) copy-start(f32[8192]{0:T(1024)} %param.12) | copy-start | bytes 98308
where the time goes:
time: 238 us; the launch traced here: 237 us
  other arithmetic  153 us (64%)
  local copies, waits for them, and re-layouts  59.1 us (25%)
  starting transfers between devices  11.2 us (5%)
  blocking collectives  10.3 us (4%)
    reduce_sum x4, other arithmetic, pair_terms(): force = jnp.sum(coeff[None] * delta, axis=-1)  62 us
    reduce_sum x4, other arithmetic, pair_terms(): dist_sq = jnp.sum(delta * delta, axis=0)  46.4 us
    gather x4, local copies, waits for them, and re-layouts, body(): pick_atoms = jax.vmap(lambda source, index: source[:, index])  41.7 us
    reduce_sum x4, other arithmetic, add_partner(): return ((carry[0] + force, carry[1] + jnp.sum(energy, axis=1)), None)  39.9 us
    psum x1, blocking collectives, body(): lax.psum((image_total(ahead * ahead), image_total(behind * behind), image...  10.3 us
    ppermute x2, starting transfers between devices, extended_2(): before = lax.ppermute(last, axis, up)  8.61 us
  transfers between devices with their start and end apart: 4, of which 0 were waited for; matrix products, arithmetic and copies ran while one was open for 88% of the time, Pallas kernels for 0%

commit v1 on v0

v1 whole, which is shorter than its diff:
```python
import jax
import jax.numpy as jnp
from jax import lax
from jax.experimental import pallas as pl
from jax.experimental.pallas import tpu as pltpu
from jax.sharding import PartitionSpec as P

TILE = 128
PARTNERS = 4

soft_core = 1.0
spring_k = 2.0
small_eps = 1e-06


def lookup(row, index):
    return jnp.take_along_axis(
        jnp.broadcast_to(row, index.shape), index, axis=1, mode="promise_in_bounds"
    )


def pair_kernel(
    lists_ref, edge_ref, coords_ref, types_ref, low_ref, low_types_ref, up_ref, up_types_ref,
    halo_ref, table_ref, force_ref, energy_ref, param_ref, feat_ref, cols_ref,
):
    images = coords_ref.shape[0]
    tiles = coords_ref.shape[2] // TILE
    halo_tiles = halo_ref.shape[2]
    wells, radii = table_ref[0:1, :], table_ref[1:2, :]
    for b in range(tiles // 8):
        kinds = types_ref[b * 8:(b + 1) * 8, :]
        param_ref[0, b * 8:(b + 1) * 8, :] = lookup(wells, kinds)
        param_ref[1, b * 8:(b + 1) * 8, :] = lookup(radii, kinds)

    for m in range(images):
        for t in range(tiles):
            feat_ref[m, t, 0:3, :] = coords_ref[m, :, t * TILE:(t + 1) * TILE]
            feat_ref[m, t, 3:4, :] = param_ref[0, t:t + 1, :]
            feat_ref[m, t, 4:5, :] = param_ref[1, t:t + 1, :]
        for side, (src, kinds) in enumerate(((low_ref, low_types_ref), (up_ref, up_types_ref))):
            index = halo_ref[m, side]
            lane = jnp.bitwise_and(index, TILE - 1)
            row = jnp.right_shift(index, 7)
            x = jnp.zeros((halo_tiles, TILE), jnp.float32)
            got = [x, x, x, jnp.zeros((halo_tiles, TILE), jnp.int32)]
            for t in range(tiles):
                hit = row == t
                for f in range(3):
                    g = lookup(src[m, f:f + 1, t * TILE:(t + 1) * TILE], lane)
                    got[f] = jnp.where(hit, g, got[f])
                got[3] = jnp.where(hit, lookup(kinds[t:t + 1, :], lane), got[3])
            inside = jnp.full((halo_tiles, TILE), edge_ref[side]) > 0
            full = got[:3] + [lookup(wells, got[3]), lookup(radii, got[3])]
            for f in range(5):
                value = jnp.where(inside, full[f], 0.0)
                for u in range(halo_tiles):
                    feat_ref[m, tiles + side * halo_tiles + u, f:f + 1, :] = value[u:u + 1, :]

    ext = tiles + 2 * halo_tiles

    def turn(n, carry):
        for m in range(images):
            cols_ref[m, n, :, 0:8] = feat_ref[m, n].T
        return carry

    lax.fori_loop(0, ext, turn, 0)

    for m in range(images):
        def tile_step(t, energy):
            own = [jnp.broadcast_to(feat_ref[m, t, f:f + 1, :], (8, TILE)) for f in range(5)]
            zero = jnp.zeros((8, TILE), jnp.float32)
            fx, fy, fz, en = zero, zero, zero, zero
            for k in range(PARTNERS):
                p = lists_ref[m, k, t]
                for j in range(TILE // 8):
                    v = cols_ref[m, p, j * 8:(j + 1) * 8, 0:8]
                    part = [jnp.broadcast_to(v[:, f:f + 1], (8, TILE)) for f in range(5)]
                    dx, dy, dz = own[0] - part[0], own[1] - part[1], own[2] - part[2]
                    reach = own[4] + part[4]
                    reach_sq = reach * reach
                    den = (dx * dx + dy * dy) + (dz * dz + reach_sq)
                    inv = pl.reciprocal(den, approx=True)
                    inv = inv * (2.0 - den * inv)
                    ratio = reach_sq * inv
                    cubed = ratio * ratio * ratio
                    a = part[3] * cubed
                    b = a * cubed
                    e = b - a
                    en = en + e
                    c = (b + e) * inv
                    fx = fx + c * dx
                    fy = fy + c * dy
                    fz = fz + c * dz
            scale = 24.0 * feat_ref[m, t, 3:4, :]
            rows = jnp.concatenate(
                [jnp.sum(f, axis=0, keepdims=True) * scale for f in (fx, fy, fz)], axis=0
            )
            force_ref[m, :, pl.ds(pl.multiple_of(t * TILE, TILE), TILE)] = rows
            return energy + 4.0 * own[3] * en

        energy_ref[m] = lax.fori_loop(0, tiles, tile_step, jnp.zeros((8, TILE), jnp.float32))


def pair_forces(lists, edge, coords, types, low, low_types, up, up_types, halo, table):
    images, _, atoms = coords.shape
    tiles = atoms // TILE
    ext = tiles + 2 * halo.shape[2]
    vmem = pl.BlockSpec(memory_space=pltpu.VMEM)
    smem = pl.BlockSpec(memory_space=pltpu.SMEM)
    return pl.pallas_call(
        pair_kernel,
        out_shape=(
            jax.ShapeDtypeStruct((images, 3, atoms), jnp.float32),
            jax.ShapeDtypeStruct((images, 8, TILE), jnp.float32),
        ),
        in_specs=[smem, smem] + [vmem] * 8,
        out_specs=(vmem, vmem),
        scratch_shapes=[
            pltpu.VMEM((2, tiles, TILE), jnp.float32),
            pltpu.VMEM((images, ext, 8, TILE), jnp.float32),
            pltpu.VMEM((images, ext, TILE, TILE), jnp.float32),
        ],
        compiler_params=pltpu.CompilerParams(vmem_limit_bytes=40 * 1024 * 1024),
    )(lists, edge, coords, types, low, low_types, up, up_types, halo, table)


def image_total(values):
    return jnp.sum(values, axis=(1, 2))


def body(
    coords, ref_coords, restraint, atom_types, well_table, radius_table, tile_lists, halo_index
):
    img_local, _, atoms_local = coords.shape
    tiles_local = atoms_local // TILE
    n_space = lax.axis_size("space")
    n_image = lax.axis_size("image")
    types = atom_types.reshape(tiles_local, TILE)
    table = jnp.pad(
        jnp.stack([well_table, radius_table]), ((0, 0), (0, TILE - well_table.shape[0]))
    )
    up = [(i, i + 1) for i in range(n_space - 1)]
    down = [(j, i) for i, j in up]
    low = lax.ppermute(coords, "space", up)
    high = lax.ppermute(coords, "space", down)
    low_types = lax.ppermute(types, "space", up)
    high_types = lax.ppermute(types, "space", down)
    up_i = [(i, i + 1) for i in range(n_image - 1)]
    down_i = [(j, i) for i, j in up_i]
    before = lax.ppermute(coords[-1:], "image", up_i)
    after = lax.ppermute(coords[:1], "image", down_i)
    slab = lax.axis_index("space")
    edge = jnp.stack([slab > 0, slab < n_space - 1]).astype(jnp.int32)
    halo = halo_index.reshape(img_local, 2, -1, TILE)
    pair_force, pair_energy = pair_forces(
        tile_lists, edge, coords, types, low, low_types, high, high_types, halo, table
    )
    offset = coords - ref_coords[None]
    forces = pair_force - restraint[None, None] * offset
    local_energy = 0.5 * image_total(pair_energy) + 0.5 * image_total(
        restraint[None, None] * offset * offset
    )
    rims = jnp.concatenate([before, coords, after], axis=0)
    ahead = rims[2:] - coords
    behind = coords - rims[:-2]
    ahead_sq, behind_sq, cross, force_ahead, force_behind, energy_sum = lax.psum(
        (
            image_total(ahead * ahead),
            image_total(behind * behind),
            image_total(ahead * behind),
            image_total(forces * ahead),
            image_total(forces * behind),
            local_energy,
        ),
        "space",
    )
    ahead_norm = jnp.sqrt(ahead_sq + small_eps)
    behind_norm = jnp.sqrt(behind_sq + small_eps)
    tan_sq = (
        ahead_sq / (ahead_norm * ahead_norm)
        + 2.0 * cross / (ahead_norm * behind_norm)
        + behind_sq / (behind_norm * behind_norm)
    )
    tan_norm = jnp.sqrt(tan_sq + small_eps)
    ahead_len = ahead_norm[:, None, None]
    behind_len = behind_norm[:, None, None]
    tan_len = tan_norm[:, None, None]
    unit = (ahead / ahead_len + behind / behind_len) / tan_len
    along = ((force_ahead / ahead_norm + force_behind / behind_norm) / tan_norm)[:, None, None]
    banded = forces - along * unit + spring_k * (ahead_len - behind_len) * unit
    total_images = img_local * n_image
    order = lax.axis_index("image") * img_local + jnp.arange(img_local, dtype=jnp.int32)
    ends = ((order == 0) | (order == total_images - 1))[:, None, None]
    neb_force = jnp.where(ends, forces, banded)
    energies = energy_sum / (atoms_local * n_space)
    return (neb_force, energies)


def solution(mesh):
    in_specs = (
        P("image", None, "space"),
        P(None, "space"),
        P("space"),
        P("space"),
        P(),
        P(),
        P("image", None, "space"),
        P("image", None, "space"),
    )
    out_specs = (P("image", None, "space"), P("image"))
    return jax.shard_map(body, mesh=mesh, in_specs=in_specs, out_specs=out_specs, check_vma=False)
```

time: 238 us -> 132 us (0.55)
  other arithmetic: 153 us -> 1.74 us
  Pallas kernels: 0 us -> 96.4 us
  local copies, waits for them, and re-layouts: 59.1 us -> 2.62 us
  starting transfers between devices: 11.2 us -> 16.5 us
  blocking collectives: 10.3 us -> 13 us
    reduce_sum x12 -> x0, other arithmetic: 148 us -> none  [the longest x4 62 us: pair_terms(): force = jnp.sum(coeff[None] * delta, axis=-1)]
    pallas_call x0 -> x1, Pallas kernels: none -> 96.4 us  [pair_forces(): pl.pallas_call(pair_kernel, out_shape=(jax.ShapeDtypeStruct((images, 3, a...]
    gather x12 -> x0, local copies, waits for them, and re-layouts: 46.1 us -> none  [the longest x4 41.7 us: body(): pick_atoms = jax.vmap(lambda source, index: source[:, index])]
    ppermute x2 -> x0, local copies, waits for them, and re-layouts: 9.3 us -> none  [the longest x1 4.65 us: extended_2(): before = lax.ppermute(last, axis, up)]
    ppermute x4 -> x6, starting transfers between devices: 11.2 us -> 16.5 us  [the longest x1 4.94 us: body(): low = lax.ppermute(coords, 'space', up)]
    psum x1, blocking collectives: 10.3 us -> 13 us  [body(): lax.psum((image_total(ahead * ahead), image_total(behind * behind), image...]
  transfers between devices with their start and end apart: 4 -> 6, of which waited for: 0 -> 0; matrix products, arithmetic and copies ran while one was open for 88% -> 0% of each run, Pallas kernels for 0% -> 73%
where the time goes in v1:
time: 132 us; the launch traced here: 131 us
  Pallas kernels  96.4 us (73%)
  starting transfers between devices  16.5 us (12%)
  blocking collectives  13 us (10%)
  local copies, waits for them, and re-layouts  2.62 us (2%)
  other arithmetic  1.74 us (1%)
    pallas_call x1, Pallas kernels, pair_forces(): pl.pallas_call(pair_kernel, out_shape=(jax.ShapeDtypeStruct((images, 3, a...  96.4 us
    psum x1, blocking collectives, body(): lax.psum((image_total(ahead * ahead), image_total(behind * behind), image...  13 us
    ppermute x1, starting transfers between devices, body(): low = lax.ppermute(coords, 'space', up)  4.94 us
    ppermute x1, starting transfers between devices, body(): low_types = lax.ppermute(types, 'space', up)  4.55 us
    ppermute x1, starting transfers between devices, body(): before = lax.ppermute(coords[-1:], 'image', up_i)  3.04 us
  transfers between devices with their start and end apart: 6, of which 0 were waited for; matrix products, arithmetic and copies ran while one was open for 0% of the time, Pallas kernels for 73%

profile of v1, /device:TPU:0, one launch (start us, length us, event | category | flops | bytes accessed | tf_op | source)
XLA Modules:
  0.0 131.2 jit_solution(11858813653740190439)
XLA Ops:
  0.6 1.1 copy.12.coords_ref
  1.7 4.9 %collective-permute-start = (f32[2,3,8192]{2,1,0:T(4,128)S(1)}, f32[2,3,8192]{2,1,0:T(4,128)S(1)}, u32[]{:S(2)}, u32[]{:S(2)}) collective-permute-start(f32[2,3,8192]{2,1,0:T(4,128)S(1)} %copy.12.coords_ref), channel_id=1, source_target_pairs={{0,1},{1,2},{2,3},{4,5},{5,6},{6,7},{8,9},{9,10},{10,11},{12,13},{... | collective-permute-start | bytes 589832 | tf_op jit(solution)/shard_map/ppermute | solution.py:144
  6.7 1.3 collective-permute-start.2
  8.0 4.5 %collective-permute-start.1 = (s32[64,128]{1,0:T(8,128)S(1)}, s32[64,128]{1,0:T(8,128)S(1)}, u32[]{:S(2)}, u32[]{:S(2)}) collective-permute-start(s32[64,128]{1,0:T(8,128)S(1)} %bitcast.5), channel_id=1, source_target_pairs={{0,1},{1,2},{2,3},{4,5},{5,6},{6,7},{8,9},{9,10},{10,11},{12,13},{... | collective-permute-start | bytes 98312 | tf_op jit(solution)/shard_map/ppermute | solution.py:146
  12.5 1.3 collective-permute-start.3
  13.9 0.0 copy-start.6
  13.9 0.0 copy-start.7
  13.9 0.0 copy-start.5
  13.9 1.4 %collective-permute-start.4 = (f32[1,3,8192]{2,1,0:T(4,128)S(1)}, f32[1,3,8192]{2,1,0:T(4,128)S(1)}, u32[]{:S(2)}, u32[]{:S(2)}) collective-permute-start(f32[1,3,8192]{2,1,0:T(4,128)S(1)} %get-tuple-element.24), channel_id=1, source_target_pairs={{4,0},{8,4},{12,8},{16,12},{20,16},{24,20},{28,24},{5,1},{9,5},{13... | collective-permute-start | bytes 294920 | tf_op jit(solution)/shard_map/ppermute | solution.py:151
  15.4 3.0 %collective-permute-start.5 = (f32[1,3,8192]{2,1,0:T(4,128)S(1)}, f32[1,3,8192]{2,1,0:T(4,128)S(1)}, u32[]{:S(2)}, u32[]{:S(2)}) collective-permute-start(f32[1,3,8192]{2,1,0:T(4,128)S(1)} %get-tuple-element.23), channel_id=1, source_target_pairs={{0,4},{4,8},{8,12},{12,16},{16,20},{20,24},{24,28},{1,5},{5,9},{9,... | collective-permute-start | bytes 294920 | tf_op jit(solution)/shard_map/ppermute | solution.py:150
  18.5 0.1 add_convert_fusion.edge_ref
  18.6 0.0 copy-start.2
  18.6 0.0 copy-start.3
  18.6 0.0 collective-permute-done.3.up_types_ref
  18.6 0.0 collective-permute-done.low_ref
  18.6 0.6 copy-done.1
  19.2 96.4 %shard_map.95 = (f32[2,3,8192]{2,1,0:T(4,128)S(1)}, f32[2,8,128]{2,1,0:T(8,128)S(1)}) custom-call(s32[2,4,64]{2,1,0:T(4,128)S(1)} %copy-done.1, s32[2]{0:T(128)S(1)} %add_convert_fusion.edge_ref, f32[2,3,8192]{2,1,0:T(4,128)S(1)} %copy.12.coords_ref, s32[64,128]{1,0:T(8,128)S(1)} %bitcast.7, f32[2,3,8192]{2,1,0:T(4,128)S(1)} %collective-permute-done.low_ref, ...), custom_call_target="tpu_custom_call" | custom-call | tf_op jit(solution)/shard_map/pallas_call | solution.py:110
  115.7 0.1 reduce_sum.68
  115.8 0.0 collective-permute-done.4
  115.8 0.7 multiply_reduce_fusion.4
  116.5 13.0 %all-reduce.1 = (f32[2]{0:T(128)S(1)}, f32[2]{0:T(128)S(1)}, f32[2]{0:T(128)S(1)}, f32[2]{0:T(128)S(1)}, f32[2]{0:T(128)S(1)}, /*index=5*/f32[2]{0:T(128)S(1)}) all-reduce(f32[2]{0:T(128)S(1)} %get-tuple-element.12, f32[2]{0:T(128)S(1)} %get-tuple-element.11, ...), channel_id=1, replica_groups=mesh['image'=8,'space'=4] {'space'}, use_global_device_ids=true, to_apply=%region_3.4 | all-reduce | flops 12 | bytes 96 | tf_op jit(solution)/shard_map/psum | solution.py:166
  129.5 0.5 add_divide_fusion
  130.1 0.3 add_select_fusion
  130.4 0.8 copy.20
  (18 shorter events, 0.1 us)
Async XLA Ops:
  0.6 7.3 %copy-start = (s32[8192]{0:T(1024)S(1)}, s32[8192]{0:T(1024)}, u32[]{:S(2)}) copy-start(s32[8192]{0:T(1024)} %param.11) | copy-start | bytes 98308
  1.7 16.9 %collective-permute-start = (f32[2,3,8192]{2,1,0:T(4,128)S(1)}, f32[2,3,8192]{2,1,0:T(4,128)S(1)}, u32[]{:S(2)}, u32[]{:S(2)}) collective-permute-start(f32[2,3,8192]{2,1,0:T(4,128)S(1)} %copy.12.coords_ref), channel_id=1, source_target_pairs={{0,1},{1,2},{2,3},{4,5},{5,6},{6,7},{8,9},{9,10},{10,11},{12,13},{... | collective-permute-start | bytes 589832 | tf_op jit(solution)/shard_map/ppermute | solution.py:144
  6.7 12.0 %collective-permute-start.2 = (f32[2,3,8192]{2,1,0:T(4,128)S(1)}, f32[2,3,8192]{2,1,0:T(4,128)S(1)}, u32[]{:S(2)}, u32[]{:S(2)}) collective-permute-start(f32[2,3,8192]{2,1,0:T(4,128)S(1)} %copy.12.coords_ref), channel_id=1, source_target_pairs={{1,0},{2,1},{3,2},{5,4},{6,5},{7,6},{9,8},{10,9},{11,10},{13,12},{... | collective-permute-start | bytes 589832 | tf_op jit(solution)/shard_map/ppermute | solution.py:145
  8.0 7.4 %collective-permute-start.1 = (s32[64,128]{1,0:T(8,128)S(1)}, s32[64,128]{1,0:T(8,128)S(1)}, u32[]{:S(2)}, u32[]{:S(2)}) collective-permute-start(s32[64,128]{1,0:T(8,128)S(1)} %bitcast.5), channel_id=1, source_target_pairs={{0,1},{1,2},{2,3},{4,5},{5,6},{6,7},{8,9},{9,10},{10,11},{12,13},{... | collective-permute-start | bytes 98312 | tf_op jit(solution)/shard_map/ppermute | solution.py:146
  12.5 6.1 %collective-permute-start.3 = (s32[64,128]{1,0:T(8,128)S(1)}, s32[64,128]{1,0:T(8,128)S(1)}, u32[]{:S(2)}, u32[]{:S(2)}) collective-permute-start(s32[64,128]{1,0:T(8,128)S(1)} %bitcast.6), channel_id=1, source_target_pairs={{1,0},{2,1},{3,2},{5,4},{6,5},{7,6},{9,8},{10,9},{11,10},{13,12},{... | collective-permute-start | bytes 98312 | tf_op jit(solution)/shard_map/ppermute | solution.py:147
  13.9 1.5 %copy-start.6 = (f32[64]{0:T(128)S(1)}, f32[64]{0:T(128)}, u32[]{:S(2)}) copy-start(f32[64]{0:T(128)} %param.13) | copy-start | bytes 772
  13.9 1.5 %copy-start.7 = (f32[64]{0:T(128)S(1)}, f32[64]{0:T(128)}, u32[]{:S(2)}) copy-start(f32[64]{0:T(128)} %param.12) | copy-start | bytes 772
  13.9 4.6 %copy-start.5 = (s32[2,2,1024]{2,1,0:T(2,128)S(1)}, s32[2,2,1024]{2,1,0:T(2,128)}, u32[]{:S(2)}) copy-start(s32[2,2,1024]{2,1,0:T(2,128)} %param.15) | copy-start | bytes 49156
  13.9 101.8 %collective-permute-start.4 = (f32[1,3,8192]{2,1,0:T(4,128)S(1)}, f32[1,3,8192]{2,1,0:T(4,128)S(1)}, u32[]{:S(2)}, u32[]{:S(2)}) collective-permute-start(f32[1,3,8192]{2,1,0:T(4,128)S(1)} %get-tuple-element.24), channel_id=1, source_target_pairs={{4,0},{8,4},{12,8},{16,12},{20,16},{24,20},{28,24},{5,1},{9,5},{13... | collective-permute-start | bytes 294920 | tf_op jit(solution)/shard_map/ppermute | solution.py:151
  15.4 100.3 %collective-permute-start.5 = (f32[1,3,8192]{2,1,0:T(4,128)S(1)}, f32[1,3,8192]{2,1,0:T(4,128)S(1)}, u32[]{:S(2)}, u32[]{:S(2)}) collective-permute-start(f32[1,3,8192]{2,1,0:T(4,128)S(1)} %get-tuple-element.23), channel_id=1, source_target_pairs={{0,4},{4,8},{8,12},{12,16},{16,20},{20,24},{24,28},{1,5},{5,9},{9,... | collective-permute-start | bytes 294920 | tf_op jit(solution)/shard_map/ppermute | solution.py:150
  18.6 0.7 copy-start.1
  18.6 97.2 %copy-start.2 = (f32[2,3,8192]{2,0,1:T(2,128)S(1)}, f32[2,3,8192]{2,0,1:T(2,128)}, u32[]{:S(2)}) copy-start(f32[2,3,8192]{2,0,1:T(2,128)} %param.8) | copy-start | bytes 589828
  18.6 97.2 %copy-start.3 = (f32[3,8192]{1,0:T(4,128)S(1)}, f32[3,8192]{1,0:T(4,128)}, u32[]{:S(2)}) copy-start(f32[3,8192]{1,0:T(4,128)} %param.9) | copy-start | bytes 294916
  19.2 96.5 %copy-start.4 = (f32[8192]{0:T(1024)S(1)}, f32[8192]{0:T(1024)}, u32[]{:S(2)}) copy-start(f32[8192]{0:T(1024)} %param.10) | copy-start | bytes 98308

commit v2 on v1

--- a/solution.py
+++ b/solution.py
@@ -1,3 +1,5 @@
+import functools
+
 import jax
 import jax.numpy as jnp
 from jax import lax
@@ -21,10 +23,10 @@
 
 def pair_kernel(
     lists_ref, edge_ref, coords_ref, types_ref, low_ref, low_types_ref, up_ref, up_types_ref,
-    halo_ref, table_ref, force_ref, energy_ref, param_ref, feat_ref, cols_ref,
+    halo_ref, table_ref, force_ref, energy_ref, param_ref, feat_ref, sums_ref,
 ):
     images = coords_ref.shape[0]
-    tiles = coords_ref.shape[2] // TILE
+    tiles = coords_ref.shape[2]
     halo_tiles = halo_ref.shape[2]
     wells, radii = table_ref[0:1, :], table_ref[1:2, :]
     for b in range(tiles // 8):
@@ -34,7 +36,8 @@
 
     for m in range(images):
         for t in range(tiles):
-            feat_ref[m, t, 0:3, :] = coords_ref[m, :, t * TILE:(t + 1) * TILE]
+            for f in range(3):
+                feat_ref[m, t, f:f + 1, :] = coords_ref[m, f, t:t + 1, :]
             feat_ref[m, t, 3:4, :] = param_ref[0, t:t + 1, :]
             feat_ref[m, t, 4:5, :] = param_ref[1, t:t + 1, :]
         for side, (src, kinds) in enumerate(((low_ref, low_types_ref), (up_ref, up_types_ref))):
@@ -46,7 +49,7 @@
             for t in range(tiles):
                 hit = row == t
                 for f in range(3):
-                    g = lookup(src[m, f:f + 1, t * TILE:(t + 1) * TILE], lane)
+                    g = lookup(src[m, f, t:t + 1, :], lane)
                     got[f] = jnp.where(hit, g, got[f])
                 got[3] = jnp.where(hit, lookup(kinds[t:t + 1, :], lane), got[3])
             inside = jnp.full((halo_tiles, TILE), edge_ref[side]) > 0
@@ -56,31 +59,25 @@
                 for u in range(halo_tiles):
                     feat_ref[m, tiles + side * halo_tiles + u, f:f + 1, :] = value[u:u + 1, :]
 
-    ext = tiles + 2 * halo_tiles
-
-    def turn(n, carry):
-        for m in range(images):
-            cols_ref[m, n, :, 0:8] = feat_ref[m, n].T
-        return carry
-
-    lax.fori_loop(0, ext, turn, 0)
-
+    sums_ref[...] = jnp.zeros_like(sums_ref)
     for m in range(images):
         def tile_step(t, energy):
-            own = [jnp.broadcast_to(feat_ref[m, t, f:f + 1, :], (8, TILE)) for f in range(5)]
-            zero = jnp.zeros((8, TILE), jnp.float32)
-            fx, fy, fz, en = zero, zero, zero, zero
-            for k in range(PARTNERS):
-                p = lists_ref[m, k, t]
-                for j in range(TILE // 8):
-                    v = cols_ref[m, p, j * 8:(j + 1) * 8, 0:8]
-                    part = [jnp.broadcast_to(v[:, f:f + 1], (8, TILE)) for f in range(5)]
+            turned = feat_ref[m, t].T
+            picks = [lists_ref[m, k, t] for k in range(PARTNERS)]
+            for i in range(TILE // 8):
+                rows = slice(i * 8, (i + 1) * 8)
+                own = [jnp.broadcast_to(turned[rows, f:f + 1], (8, TILE)) for f in range(5)]
+                zero = jnp.zeros((8, TILE), jnp.float32)
+                fx, fy, fz, en = zero, zero, zero, zero
+                for p in picks:
+                    part = [
+                        jnp.broadcast_to(feat_ref[m, p, f:f + 1, :], (8, TILE)) for f in range(5)
+                    ]
                     dx, dy, dz = own[0] - part[0], own[1] - part[1], own[2] - part[2]
                     reach = own[4] + part[4]
                     reach_sq = reach * reach
                     den = (dx * dx + dy * dy) + (dz * dz + reach_sq)
-                    inv = pl.reciprocal(den, approx=True)
-                    inv = inv * (2.0 - den * inv)
+                    inv = pltpu.reciprocal(den, approx=True)
                     ratio = reach_sq * inv
                     cubed = ratio * ratio * ratio
                     a = part[3] * cubed
@@ -91,19 +88,93 @@
                     fx = fx + c * dx
                     fy = fy + c * dy
                     fz = fz + c * dz
-            scale = 24.0 * feat_ref[m, t, 3:4, :]
-            rows = jnp.concatenate(
-                [jnp.sum(f, axis=0, keepdims=True) * scale for f in (fx, fy, fz)], axis=0
+                energy = energy + own[3] * en
+                for f, value in enumerate((fx, fy, fz)):
+                    sums_ref[rows, f:f + 1] = jnp.sum(value, axis=1, keepdims=True)
+            out = (24.0 * feat_ref[m, t, 3:4, :]) * sums_ref[...].T[0:3, :]
+            force_ref[m, :, pl.ds(pl.multiple_of(t * TILE, TILE), TILE)] = out
+            return energy
+
+        energy_ref[m] = 4.0 * lax.fori_loop(
+            0, tiles, tile_step, jnp.zeros((8, TILE), jnp.float32)
+        )
+
+
+def exchange_kernel(
+    n_space, n_image, coords_ref, types_ref, low_ref, low_types_ref, up_ref, up_types_ref,
+    before_ref, after_ref, send_sem, recv_sem,
+):
+    slab, image = lax.axis_index("space"), lax.axis_index("image")
+    last = coords_ref.shape[0] - 1
+    links = (
+        (slab < n_space - 1, slab > 0, "space", slab, 1,
+         ((coords_ref, low_ref), (types_ref, low_types_ref))),
+        (slab > 0, slab < n_space - 1, "space", slab, -1,
+         ((coords_ref, up_ref), (types_ref, up_types_ref))),
+        (image < n_image - 1, image > 0, "image", image, 1,
+         ((coords_ref.at[pl.ds(last, 1)], before_ref),)),
+        (image > 0, image < n_image - 1, "image", image, -1,
+         ((coords_ref.at[pl.ds(0, 1)], after_ref),)),
+    )
+    barrier = pltpu.get_barrier_semaphore()
+    for sends, _, axis, here, step, _ in links:
+        @pl.when(sends)
+        def _(axis=axis, here=here, step=step):
+            pl.semaphore_signal(
+                barrier, inc=1, device_id={axis: here + step}, device_id_type=pl.DeviceIdType.MESH
             )
-            force_ref[m, :, pl.ds(pl.multiple_of(t * TILE, TILE), TILE)] = rows
-            return energy + 4.0 * own[3] * en
-
-        energy_ref[m] = lax.fori_loop(0, tiles, tile_step, jnp.zeros((8, TILE), jnp.float32))
+    peers = sum(link[0].astype(jnp.int32) for link in links)
+    pl.semaphore_wait(barrier, peers)
+
+    slot = 0
+    waits = []
+    for sends, gets, axis, here, step, pairs in links:
+        copies = []
+        for src, dst in pairs:
+            copies.append(pltpu.make_async_remote_copy(
+                src_ref=src, dst_ref=dst, send_sem=send_sem.at[slot], recv_sem=recv_sem.at[slot],
+                device_id={axis: here + step}, device_id_type=pl.DeviceIdType.MESH,
+            ))
+            slot += 1
+        @pl.when(sends)
+        def _(copies=copies):
+            for c in copies:
+                c.start()
+        @pl.when(jnp.logical_not(gets))
+        def _(pairs=pairs):
+            for _, dst in pairs:
+                dst[...] = jnp.zeros_like(dst)
+        waits.append((sends, gets, copies))
+    for sends, gets, copies in waits:
+        @pl.when(gets)
+        def _(copies=copies):
+            for c in copies:
+                c.wait_recv()
+    for sends, gets, copies in waits:
+        @pl.when(sends)
+        def _(copies=copies):
+            for c in copies:
+                c.wait_send()
+
+
+def exchange(coords, types, n_space, n_image):
+    vmem = pl.BlockSpec(memory_space=pltpu.VMEM)
+    whole = jax.ShapeDtypeStruct(coords.shape, coords.dtype)
+    kinds = jax.ShapeDtypeStruct(types.shape, types.dtype)
+    rim = jax.ShapeDtypeStruct((1,) + coords.shape[1:], coords.dtype)
+    return pl.pallas_call(
+        functools.partial(exchange_kernel, n_space, n_image),
+        out_shape=(whole, kinds, whole, kinds, rim, rim),
+        in_specs=[vmem, vmem],
+        out_specs=(vmem,) * 6,
+        scratch_shapes=[pltpu.SemaphoreType.DMA((6,)), pltpu.SemaphoreType.DMA((6,))],
+        compiler_params=pltpu.CompilerParams(collective_id=0, has_side_effects=True),
+    )(coords, types)
 
 
 def pair_forces(lists, edge, coords, types, low, low_types, up, up_types, halo, table):
-    images, _, atoms = coords.shape
-    tiles = atoms // TILE
+    images, _, tiles, _ = coords.shape
+    atoms = tiles * TILE
     ext = tiles + 2 * halo.shape[2]
     vmem = pl.BlockSpec(memory_space=pltpu.VMEM)
     smem = pl.BlockSpec(memory_space=pltpu.SMEM)
@@ -118,7 +189,7 @@
         scratch_shapes=[
             pltpu.VMEM((2, tiles, TILE), jnp.float32),
             pltpu.VMEM((images, ext, 8, TILE), jnp.float32),
-            pltpu.VMEM((images, ext, TILE, TILE), jnp.float32),
+            pltpu.VMEM((TILE, 8), jnp.float32),
         ],
         compiler_params=pltpu.CompilerParams(vmem_limit_bytes=40 * 1024 * 1024),
     )(lists, edge, coords, types, low, low_types, up, up_types, halo, table)
@@ -139,21 +210,15 @@
     table = jnp.pad(
         jnp.stack([well_table, radius_table]), ((0, 0), (0, TILE - well_table.shape[0]))
     )
-    up = [(i, i + 1) for i in range(n_space - 1)]
-    down = [(j, i) for i, j in up]
-    low = lax.ppermute(coords, "space", up)
-    high = lax.ppermute(coords, "space", down)
-    low_types = lax.ppermute(types, "space", up)
-    high_types = lax.ppermute(types, "space", down)
-    up_i = [(i, i + 1) for i in range(n_image - 1)]
-    down_i = [(j, i) for i, j in up_i]
-    before = lax.ppermute(coords[-1:], "image", up_i)
-    after = lax.ppermute(coords[:1], "image", down_i)
+    tiled = coords.reshape(img_local, 3, tiles_local, TILE)
+    low, low_types, high, high_types, before, after = exchange(tiled, types, n_space, n_image)
+    before = before.reshape(1, 3, atoms_local)
+    after = after.reshape(1, 3, atoms_local)
     slab = lax.axis_index("space")
     edge = jnp.stack([slab > 0, slab < n_space - 1]).astype(jnp.int32)
     halo = halo_index.reshape(img_local, 2, -1, TILE)
     pair_force, pair_energy = pair_forces(
-        tile_lists, edge, coords, types, low, low_types, high, high_types, halo, table
+        tile_lists, edge, tiled, types, low, low_types, high, high_types, halo, table
     )
     offset = coords - ref_coords[None]
     forces = pair_force - restraint[None, None] * offset

time: 132 us -> 215 us (1.63)
  Pallas kernels: 96.4 us -> 193 us
  starting transfers between devices: 16.5 us -> 0 us
  local copies, waits for them, and re-layouts: 2.62 us -> 8.5 us
  blocking collectives: 13 us -> 10.8 us
    pallas_call x1, Pallas kernels: 96.4 us -> 181 us  [pair_forces(): pl.pallas_call(pair_kernel, out_shape=(jax.ShapeDtypeStruct((images, 3, a...]
    ppermute x6 -> x0, starting transfers between devices: 16.5 us -> none  [the longest x1 4.94 us: body(): low = lax.ppermute(coords, 'space', up)]
    pallas_call x0 -> x1, Pallas kernels: none -> 12.3 us  [exchange(): pl.pallas_call(functools.partial(exchange_kernel, n_space, n_image), out_...]
    unnamed x18 -> x32, local copies, waits for them, and re-layouts: 2.55 us -> 6.55 us
    psum x1, blocking collectives: 13 us -> 10.8 us  [body(): lax.psum((image_total(ahead * ahead), image_total(behind * behind), image...]
  transfers between devices with their start and end apart: 6 -> 0, of which waited for: 0 -> 0; matrix products, arithmetic and copies ran while one was open for 0% -> 0% of each run, Pallas kernels for 73% -> 0%
where the time goes in v2:
time: 215 us
  Pallas kernels  193 us (90%)
  blocking collectives  10.8 us (5%)
  local copies, waits for them, and re-layouts  8.5 us (4%)
    pallas_call x1, Pallas kernels, pair_forces(): pl.pallas_call(pair_kernel, out_shape=(jax.ShapeDtypeStruct((images, 3, a...  181 us
    pallas_call x1, Pallas kernels, exchange(): pl.pallas_call(functools.partial(exchange_kernel, n_space, n_image), out_...  12.3 us
    psum x1, blocking collectives, body(): lax.psum((image_total(ahead * ahead), image_total(behind * behind), image...  10.8 us
    unnamed x32, local copies, waits for them, and re-layouts  6.55 us

profile of v2, /device:TPU:0, one launch (start us, length us, event | category | flops | bytes accessed | tf_op | source)
XLA Modules:
  0.0 214.8 jit_solution(11735351728398938462)
XLA Ops:
  0.6 1.1 reshape.35
  1.7 0.7 copy.18.coords_ref
  2.4 12.3 %shard_map.95 = (f32[2,3,64,128]{3,2,1,0:T(8,128)}, s32[64,128]{1,0:T(8,128)}, f32[2,3,64,128]{3,2,1,0:T(8,128)}, s32[64,128]{1,0:T(8,128)}, f32[1,3,64,128]{3,2,1,0:T(8,128)}, /*index=5*/f32[1,3,64,128]{3,2,1,0:T(8,128)}) custom-call(f32[2,3,64,128]{3,2,1,0:T(8,128)} %copy.18.coords_ref, s32[64,128]{1,0:T(8,128)} %bitcast.9), custom_call_target="tpu_custom_call" | custom-call | tf_op jit(solution)/shard_map/pallas_call | solution.py:165
  14.8 0.0 copy-start.3
  14.8 0.1 add_convert_fusion.edge_ref
  14.9 0.6 copy-done.13
  15.5 0.0 copy-done.14
  15.6 0.0 copy-done.6
  15.6 0.9 copy-done.1
  16.5 0.9 copy-done.2
  17.4 0.8 copy-done.4
  18.2 0.8 copy-done.5
  19.0 180.7 %shard_map.96 = (f32[2,3,8192]{2,1,0:T(4,128)S(1)}, f32[2,8,128]{2,1,0:T(8,128)S(1)}) custom-call(s32[2,4,64]{2,1,0:T(4,128)S(1)} %copy-done.6, s32[2]{0:T(128)S(1)} %add_convert_fusion.edge_ref, f32[2,3,64,128]{3,2,1,0:T(8,128)S(1)} %copy-done, s32[64,128]{1,0:T(8,128)S(1)} %bitcast.10, f32[2,3,64,128]{3,2,1,0:T(8,128)S(1)} %copy-done.1, ...), custom_call_target="tpu_custom_call" | custom-call | tf_op jit(solution)/shard_map/pallas_call | solution.py:181
  199.7 0.1 copy.21
  199.8 0.1 copy.23
  199.9 0.8 copy-done.7
  200.6 0.1 copy.19
  200.8 0.8 copy-done.8
  201.5 0.7 multiply_reduce_fusion.4
  202.3 0.1 reduce_sum.68
  202.4 10.8 %all-reduce.1 = (f32[2]{0:T(128)S(1)}, f32[2]{0:T(128)S(1)}, f32[2]{0:T(128)S(1)}, f32[2]{0:T(128)S(1)}, f32[2]{0:T(128)S(1)}, /*index=5*/f32[2]{0:T(128)S(1)}) all-reduce(f32[2]{0:T(128)S(1)} %get-tuple-element.26, f32[2]{0:T(128)S(1)} %get-tuple-element.25, ...), channel_id=1, replica_groups=mesh['image'=8,'space'=4] {'space'}, use_global_device_ids=true, to_apply=%region_3.4 | all-reduce | flops 12 | bytes 96 | tf_op jit(solution)/shard_map/psum | solution.py:231
  213.2 0.5 add_divide_fusion
  213.7 0.3 add_select_fusion
  214.0 0.8 copy.26
  (24 shorter events, 0.1 us)
Async XLA Ops:
  2.4 13.1 %copy-start = (f32[2,3,64,128]{3,2,1,0:T(8,128)S(1)}, f32[2,3,64,128]{3,2,1,0:T(8,128)}, u32[]{:S(2)}) copy-start(f32[2,3,64,128]{3,2,1,0:T(8,128)} %copy.18.coords_ref) | copy-start | bytes 589828
  2.4 12.4 %copy-start.12 = (s32[2,2,1024]{2,1,0:T(2,128)S(1)}, s32[2,2,1024]{2,1,0:T(2,128)}, u32[]{:S(2)}) copy-start(s32[2,2,1024]{2,1,0:T(2,128)} %param.15) | copy-start | bytes 49156
  14.8 0.8 copy-start.3
  14.9 0.7 copy-start.13
  14.9 0.7 copy-start.14
  14.9 0.7 copy-start.6
  15.6 0.9 copy-start.1
  16.5 0.9 copy-start.2
  17.4 0.8 copy-start.4
  18.2 0.8 copy-start.5
  19.0 180.7 %copy-start.10 = (f32[1,3,64,128]{3,2,1,0:T(8,128)S(1)}, f32[1,3,64,128]{3,2,1,0:T(8,128)}, u32[]{:S(2)}) copy-start(f32[1,3,64,128]{3,2,1,0:T(8,128)} %get-tuple-element.15) | copy-start | bytes 294916
  19.0 180.8 %copy-start.9 = (f32[1,3,64,128]{3,2,1,0:T(8,128)S(1)}, f32[1,3,64,128]{3,2,1,0:T(8,128)}, u32[]{:S(2)}) copy-start(f32[1,3,64,128]{3,2,1,0:T(8,128)} %get-tuple-element.16) | copy-start | bytes 294916
  199.7 0.9 copy-start.7
  200.6 0.9 copy-start.8
  200.6 0.9 copy-start.11

commit v3 on v2

--- a/solution.py
+++ b/solution.py
@@ -23,7 +23,7 @@
 
 def pair_kernel(
     lists_ref, edge_ref, coords_ref, types_ref, low_ref, low_types_ref, up_ref, up_types_ref,
-    halo_ref, table_ref, force_ref, energy_ref, param_ref, feat_ref, sums_ref,
+    halo_ref, table_ref, force_ref, energy_ref, param_ref, feat_ref, cols_ref,
 ):
     images = coords_ref.shape[0]
     tiles = coords_ref.shape[2]
@@ -59,20 +59,24 @@
                 for u in range(halo_tiles):
                     feat_ref[m, tiles + side * halo_tiles + u, f:f + 1, :] = value[u:u + 1, :]
 
-    sums_ref[...] = jnp.zeros_like(sums_ref)
+    ext = tiles + 2 * halo_tiles
     for m in range(images):
+        def spread(n, carry):
+            turned = feat_ref[m, n].T
+            for f in range(5):
+                cols_ref[f, n] = jnp.broadcast_to(turned[:, f:f + 1], (TILE, TILE))
+            return carry
+
+        lax.fori_loop(0, ext, spread, 0)
+
         def tile_step(t, energy):
-            turned = feat_ref[m, t].T
-            picks = [lists_ref[m, k, t] for k in range(PARTNERS)]
-            for i in range(TILE // 8):
-                rows = slice(i * 8, (i + 1) * 8)
-                own = [jnp.broadcast_to(turned[rows, f:f + 1], (8, TILE)) for f in range(5)]
-                zero = jnp.zeros((8, TILE), jnp.float32)
-                fx, fy, fz, en = zero, zero, zero, zero
-                for p in picks:
-                    part = [
-                        jnp.broadcast_to(feat_ref[m, p, f:f + 1, :], (8, TILE)) for f in range(5)
-                    ]
+            own = [jnp.broadcast_to(feat_ref[m, t, f:f + 1, :], (8, TILE)) for f in range(5)]
+            zero = jnp.zeros((8, TILE), jnp.float32)
+            fx, fy, fz, en = zero, zero, zero, zero
+            for k in range(PARTNERS):
+                p = lists_ref[m, k, t]
+                for j in range(TILE // 8):
+                    part = [cols_ref[f, p, j * 8:(j + 1) * 8, :] for f in range(5)]
                     dx, dy, dz = own[0] - part[0], own[1] - part[1], own[2] - part[2]
                     reach = own[4] + part[4]
                     reach_sq = reach * reach
@@ -88,16 +92,13 @@
                     fx = fx + c * dx
                     fy = fy + c * dy
                     fz = fz + c * dz
-                energy = energy + own[3] * en
-                for f, value in enumerate((fx, fy, fz)):
-                    sums_ref[rows, f:f + 1] = jnp.sum(value, axis=1, keepdims=True)
-            out = (24.0 * feat_ref[m, t, 3:4, :]) * sums_ref[...].T[0:3, :]
-            force_ref[m, :, pl.ds(pl.multiple_of(t * TILE, TILE), TILE)] = out
-            return energy
-
-        energy_ref[m] = 4.0 * lax.fori_loop(
-            0, tiles, tile_step, jnp.zeros((8, TILE), jnp.float32)
-        )
+            scale = 24.0 * feat_ref[m, t, 3:4, :]
+            force_ref[m, :, pl.ds(pl.multiple_of(t * TILE, TILE), TILE)] = jnp.concatenate(
+                [jnp.sum(f, axis=0, keepdims=True) * scale for f in (fx, fy, fz)], axis=0
+            )
+            return energy + 4.0 * own[3] * en
+
+        energy_ref[m] = lax.fori_loop(0, tiles, tile_step, jnp.zeros((8, TILE), jnp.float32))
 
 
 def exchange_kernel(
@@ -189,7 +190,7 @@
         scratch_shapes=[
             pltpu.VMEM((2, tiles, TILE), jnp.float32),
             pltpu.VMEM((images, ext, 8, TILE), jnp.float32),
-            pltpu.VMEM((TILE, 8), jnp.float32),
+            pltpu.VMEM((5, ext, TILE, TILE), jnp.float32),
         ],
         compiler_params=pltpu.CompilerParams(vmem_limit_bytes=40 * 1024 * 1024),
     )(lists, edge, coords, types, low, low_types, up, up_types, halo, table)

time: 215 us -> 111 us (0.52)
  Pallas kernels: 193 us -> 89.1 us
    pallas_call x1, Pallas kernels: 181 us -> 76.7 us  [pair_forces(): pl.pallas_call(pair_kernel, out_shape=(jax.ShapeDtypeStruct((images, 3, a...]
where the time goes in v3:
time: 111 us
  Pallas kernels  89.1 us (80%)
  blocking collectives  10.8 us (10%)
  local copies, waits for them, and re-layouts  8.5 us (8%)
  other arithmetic  1.74 us (2%)
    pallas_call x1, Pallas kernels, pair_forces(): pl.pallas_call(pair_kernel, out_shape=(jax.ShapeDtypeStruct((images, 3, a...  76.7 us
    pallas_call x1, Pallas kernels, exchange(): pl.pallas_call(functools.partial(exchange_kernel, n_space, n_image), out_...  12.3 us
    psum x1, blocking collectives, body(): lax.psum((image_total(ahead * ahead), image_total(behind * behind), image...  10.8 us
    unnamed x32, local copies, waits for them, and re-layouts  6.55 us

profile of v3, /device:TPU:0, one launch (start us, length us, event | category | flops | bytes accessed | tf_op | source)
XLA Modules:
  0.0 110.9 jit_solution(16952764445864334772)
XLA Ops:
  0.6 1.1 reshape.35
  1.7 0.7 copy.18.coords_ref
  2.4 12.3 %shard_map.95 = (f32[2,3,64,128]{3,2,1,0:T(8,128)}, s32[64,128]{1,0:T(8,128)}, f32[2,3,64,128]{3,2,1,0:T(8,128)}, s32[64,128]{1,0:T(8,128)}, f32[1,3,64,128]{3,2,1,0:T(8,128)}, /*index=5*/f32[1,3,64,128]{3,2,1,0:T(8,128)}) custom-call(f32[2,3,64,128]{3,2,1,0:T(8,128)} %copy.18.coords_ref, s32[64,128]{1,0:T(8,128)} %bitcast.9), custom_call_target="tpu_custom_call" | custom-call | tf_op jit(solution)/shard_map/pallas_call | solution.py:166
  14.8 0.1 add_convert_fusion.edge_ref
  14.9 0.0 copy-start.6
  14.9 0.6 copy-done.13
  15.5 0.0 copy-done.14
  15.6 0.0 copy-done.6
  15.6 0.9 copy-done.1
  16.5 0.9 copy-done.2
  17.4 0.8 copy-done.4
  18.2 0.8 copy-done.5
  19.0 76.7 %shard_map.96 = (f32[2,3,8192]{2,1,0:T(4,128)S(1)}, f32[2,8,128]{2,1,0:T(8,128)S(1)}) custom-call(s32[2,4,64]{2,1,0:T(4,128)S(1)} %copy-done.6, s32[2]{0:T(128)S(1)} %add_convert_fusion.edge_ref, f32[2,3,64,128]{3,2,1,0:T(8,128)S(1)} %copy-done, s32[64,128]{1,0:T(8,128)S(1)} %bitcast.10, f32[2,3,64,128]{3,2,1,0:T(8,128)S(1)} %copy-done.1, ...), custom_call_target="tpu_custom_call" | custom-call | tf_op jit(solution)/shard_map/pallas_call | solution.py:182
  95.7 0.1 copy.21
  95.8 0.1 copy.23
  95.9 0.8 copy-done.7
  96.7 0.1 copy.19
  96.8 0.8 copy-done.8
  97.6 0.7 multiply_reduce_fusion.4
  98.3 0.1 reduce_sum.68
  98.4 10.8 %all-reduce.1 = (f32[2]{0:T(128)S(1)}, f32[2]{0:T(128)S(1)}, f32[2]{0:T(128)S(1)}, f32[2]{0:T(128)S(1)}, f32[2]{0:T(128)S(1)}, /*index=5*/f32[2]{0:T(128)S(1)}) all-reduce(f32[2]{0:T(128)S(1)} %get-tuple-element.26, f32[2]{0:T(128)S(1)} %get-tuple-element.25, ...), channel_id=1, replica_groups=mesh['image'=8,'space'=4] {'space'}, use_global_device_ids=true, to_apply=%region_3.4 | all-reduce | flops 12 | bytes 96 | tf_op jit(solution)/shard_map/psum | solution.py:232
  109.2 0.5 add_divide_fusion
  109.8 0.3 add_select_fusion
  110.0 0.8 copy.26
  (24 shorter events, 0.1 us)
Async XLA Ops:
  2.4 13.1 %copy-start = (f32[2,3,64,128]{3,2,1,0:T(8,128)S(1)}, f32[2,3,64,128]{3,2,1,0:T(8,128)}, u32[]{:S(2)}) copy-start(f32[2,3,64,128]{3,2,1,0:T(8,128)} %copy.18.coords_ref) | copy-start | bytes 589828
  2.4 12.4 %copy-start.12 = (s32[2,2,1024]{2,1,0:T(2,128)S(1)}, s32[2,2,1024]{2,1,0:T(2,128)}, u32[]{:S(2)}) copy-start(s32[2,2,1024]{2,1,0:T(2,128)} %param.15) | copy-start | bytes 49156
  14.8 0.8 copy-start.3
  14.9 0.7 copy-start.13
  14.9 0.7 copy-start.14
  14.9 0.7 copy-start.6
  15.6 0.9 copy-start.1
  16.5 0.9 copy-start.2
  17.4 0.8 copy-start.4
  18.2 0.8 copy-start.5
  19.0 76.8 %copy-start.10 = (f32[1,3,64,128]{3,2,1,0:T(8,128)S(1)}, f32[1,3,64,128]{3,2,1,0:T(8,128)}, u32[]{:S(2)}) copy-start(f32[1,3,64,128]{3,2,1,0:T(8,128)} %get-tuple-element.15) | copy-start | bytes 294916
  19.0 76.9 %copy-start.9 = (f32[1,3,64,128]{3,2,1,0:T(8,128)S(1)}, f32[1,3,64,128]{3,2,1,0:T(8,128)}, u32[]{:S(2)}) copy-start(f32[1,3,64,128]{3,2,1,0:T(8,128)} %get-tuple-element.16) | copy-start | bytes 294916
  95.7 0.9 copy-start.7
  96.7 0.9 copy-start.8
  96.7 0.9 copy-start.11

commit v4 on v3

--- a/solution.py
+++ b/solution.py
@@ -27,7 +27,7 @@
 ):
     images = coords_ref.shape[0]
     tiles = coords_ref.shape[2]
-    halo_tiles = halo_ref.shape[2]
+    halo_tiles = halo_ref.shape[2] // TILE
     wells, radii = table_ref[0:1, :], table_ref[1:2, :]
     for b in range(tiles // 8):
         kinds = types_ref[b * 8:(b + 1) * 8, :]
@@ -41,23 +41,36 @@
             feat_ref[m, t, 3:4, :] = param_ref[0, t:t + 1, :]
             feat_ref[m, t, 4:5, :] = param_ref[1, t:t + 1, :]
         for side, (src, kinds) in enumerate(((low_ref, low_types_ref), (up_ref, up_types_ref))):
-            index = halo_ref[m, side]
+            index = halo_ref[m, side:side + 1, :]
             lane = jnp.bitwise_and(index, TILE - 1)
             row = jnp.right_shift(index, 7)
-            x = jnp.zeros((halo_tiles, TILE), jnp.float32)
-            got = [x, x, x, jnp.zeros((halo_tiles, TILE), jnp.int32)]
-            for t in range(tiles):
-                hit = row == t
-                for f in range(3):
-                    g = lookup(src[m, f, t:t + 1, :], lane)
-                    got[f] = jnp.where(hit, g, got[f])
-                got[3] = jnp.where(hit, lookup(kinds[t:t + 1, :], lane), got[3])
-            inside = jnp.full((halo_tiles, TILE), edge_ref[side]) > 0
-            full = got[:3] + [lookup(wells, got[3]), lookup(radii, got[3])]
-            for f in range(5):
-                value = jnp.where(inside, full[f], 0.0)
-                for u in range(halo_tiles):
-                    feat_ref[m, tiles + side * halo_tiles + u, f:f + 1, :] = value[u:u + 1, :]
+            width = index.shape[1]
+            pick = lax.broadcasted_iota(jnp.int32, (TILE, width), 0) == lane
+            pick = jnp.where(pick, 1.0, 0.0).astype(jnp.bfloat16)
+            hit = lax.broadcasted_iota(jnp.int32, (tiles, width), 0) == row
+
+            def choose(piece):
+                found = jnp.dot(piece, pick, preferred_element_type=jnp.float32)
+                return jnp.sum(jnp.where(hit, found, 0.0), axis=0, keepdims=True)
+
+            got = []
+            for f in range(3):
+                x = src[m, f]
+                high = x.astype(jnp.bfloat16)
+                rest = x - high.astype(jnp.float32)
+                mid = rest.astype(jnp.bfloat16)
+                low = (rest - mid.astype(jnp.float32)).astype(jnp.bfloat16)
+                got.append((choose(high) + choose(mid)) + choose(low))
+            which = choose(kinds[...].astype(jnp.float32).astype(jnp.bfloat16))
+            for u in range(halo_tiles):
+                part = slice(u * TILE, (u + 1) * TILE)
+                spot = tiles + side * halo_tiles + u
+                kind = jnp.broadcast_to(which[:, part].astype(jnp.int32), (8, TILE))
+                values = [g[:, part] for g in got]
+                values += [lookup(wells, kind)[0:1], lookup(radii, kind)[0:1]]
+                inside = jnp.full((1, TILE), edge_ref[side]) > 0
+                for f in range(5):
+                    feat_ref[m, spot, f:f + 1, :] = jnp.where(inside, values[f], 0.0)
 
     ext = tiles + 2 * halo_tiles
     for m in range(images):
@@ -176,7 +189,7 @@
 def pair_forces(lists, edge, coords, types, low, low_types, up, up_types, halo, table):
     images, _, tiles, _ = coords.shape
     atoms = tiles * TILE
-    ext = tiles + 2 * halo.shape[2]
+    ext = tiles + 2 * (halo.shape[2] // TILE)
     vmem = pl.BlockSpec(memory_space=pltpu.VMEM)
     smem = pl.BlockSpec(memory_space=pltpu.SMEM)
     return pl.pallas_call(
@@ -217,7 +230,7 @@
     after = after.reshape(1, 3, atoms_local)
     slab = lax.axis_index("space")
     edge = jnp.stack([slab > 0, slab < n_space - 1]).astype(jnp.int32)
-    halo = halo_index.reshape(img_local, 2, -1, TILE)
+    halo = halo_index
     pair_force, pair_energy = pair_forces(
         tile_lists, edge, tiled, types, low, low_types, high, high_types, halo, table
     )

time: 111 us -> 112 us (level)
  no operation moved by 1% of the time
where the time goes in v4:
time: 112 us
  Pallas kernels  90.1 us (80%)
  blocking collectives  10.8 us (10%)
  local copies, waits for them, and re-layouts  8.48 us (8%)
  other arithmetic  1.74 us (2%)
    pallas_call x1, Pallas kernels, pair_forces(): pl.pallas_call(pair_kernel, out_shape=(jax.ShapeDtypeStruct((images, 3, a...  77.8 us
    pallas_call x1, Pallas kernels, exchange(): pl.pallas_call(functools.partial(exchange_kernel, n_space, n_image), out_...  12.3 us
    psum x1, blocking collectives, body(): lax.psum((image_total(ahead * ahead), image_total(behind * behind), image...  10.8 us
    unnamed x32, local copies, waits for them, and re-layouts  6.55 us

profile of v4, /device:TPU:0, one launch (start us, length us, event | category | flops | bytes accessed | tf_op | source)
XLA Modules:
  0.0 111.9 jit_solution(9541768590508571483)
XLA Ops:
  0.6 1.1 reshape.32
  1.7 0.7 copy.18.coords_ref
  2.4 12.3 %shard_map.95 = (f32[2,3,64,128]{3,2,1,0:T(8,128)}, s32[64,128]{1,0:T(8,128)}, f32[2,3,64,128]{3,2,1,0:T(8,128)}, s32[64,128]{1,0:T(8,128)}, f32[1,3,64,128]{3,2,1,0:T(8,128)}, /*index=5*/f32[1,3,64,128]{3,2,1,0:T(8,128)}) custom-call(f32[2,3,64,128]{3,2,1,0:T(8,128)} %copy.18.coords_ref, s32[64,128]{1,0:T(8,128)} %bitcast.9), custom_call_target="tpu_custom_call" | custom-call | tf_op jit(solution)/shard_map/pallas_call | solution.py:179
  14.8 0.0 copy-start.6
  14.8 0.0 copy-start.7
  14.8 0.1 add_convert_fusion.edge_ref
  14.9 0.7 copy-done.13
  15.5 0.0 copy-done.14
  15.6 0.9 copy-done.1
  16.5 0.9 copy-done.2
  17.4 0.8 copy-done.4
  18.2 0.8 copy-done.5
  19.0 77.8 %shard_map.96 = (f32[2,3,8192]{2,1,0:T(4,128)S(1)}, f32[2,8,128]{2,1,0:T(8,128)S(1)}) custom-call(s32[2,4,64]{2,1,0:T(4,128)S(1)} %copy-done.7, s32[2]{0:T(128)S(1)} %add_convert_fusion.edge_ref, f32[2,3,64,128]{3,2,1,0:T(8,128)S(1)} %copy-done, s32[64,128]{1,0:T(8,128)S(1)} %bitcast.10, f32[2,3,64,128]{3,2,1,0:T(8,128)S(1)} %copy-done.1, ...), custom_call_target="tpu_custom_call" | custom-call | tf_op jit(solution)/shard_map/pallas_call | solution.py:195
  96.8 0.1 copy.21
  96.9 0.1 copy.23
  96.9 0.8 copy-done.8
  97.7 0.1 copy.19
  97.8 0.8 copy-done.9
  98.6 0.7 multiply_reduce_fusion.4
  99.3 0.1 reduce_sum.68
  99.5 10.8 %all-reduce.1 = (f32[2]{0:T(128)S(1)}, f32[2]{0:T(128)S(1)}, f32[2]{0:T(128)S(1)}, f32[2]{0:T(128)S(1)}, f32[2]{0:T(128)S(1)}, /*index=5*/f32[2]{0:T(128)S(1)}) all-reduce(f32[2]{0:T(128)S(1)} %get-tuple-element.26, f32[2]{0:T(128)S(1)} %get-tuple-element.25, ...), channel_id=1, replica_groups=mesh['image'=8,'space'=4] {'space'}, use_global_device_ids=true, to_apply=%region_3.4 | all-reduce | flops 12 | bytes 96 | tf_op jit(solution)/shard_map/psum | solution.py:245
  110.3 0.5 add_divide_fusion
  110.8 0.3 add_select_fusion
  111.1 0.8 copy.26
  (23 shorter events, 0.1 us)
Async XLA Ops:
  2.4 13.1 %copy-start = (f32[2,3,64,128]{3,2,1,0:T(8,128)S(1)}, f32[2,3,64,128]{3,2,1,0:T(8,128)}, u32[]{:S(2)}) copy-start(f32[2,3,64,128]{3,2,1,0:T(8,128)} %copy.18.coords_ref) | copy-start | bytes 589828
  2.4 13.1 %copy-start.3 = (s32[8192]{0:T(1024)S(1)}, s32[8192]{0:T(1024)}, u32[]{:S(2)}) copy-start(s32[8192]{0:T(1024)} %param.11) | copy-start | bytes 98308
  14.8 0.8 copy-start.6
  14.8 0.8 copy-start.7
  14.9 0.7 copy-start.13
  14.9 0.7 copy-start.14
  15.6 0.9 copy-start.1
  16.5 0.9 copy-start.2
  17.4 0.8 copy-start.4
  18.2 0.8 copy-start.5
  19.0 77.8 %copy-start.11 = (f32[1,3,64,128]{3,2,1,0:T(8,128)S(1)}, f32[1,3,64,128]{3,2,1,0:T(8,128)}, u32[]{:S(2)}) copy-start(f32[1,3,64,128]{3,2,1,0:T(8,128)} %get-tuple-element.15) | copy-start | bytes 294916
  19.0 77.9 %copy-start.10 = (f32[1,3,64,128]{3,2,1,0:T(8,128)S(1)}, f32[1,3,64,128]{3,2,1,0:T(8,128)}, u32[]{:S(2)}) copy-start(f32[1,3,64,128]{3,2,1,0:T(8,128)} %get-tuple-element.16) | copy-start | bytes 294916
  96.8 0.9 copy-start.8
  97.7 0.9 copy-start.9
  97.7 0.9 copy-start.12
